TPU v7x, 32 devices: a whole 2x2x4 slice. The times are simulated.
32 devices in a mesh: group: 2 (over y), stn: 4 (over z), tm: 2 (over x), pol: 2 (over core).
Axes of the slice: x: 2, y: 2, z: 4, core: 2. Of those that a mesh axis runs over, the one named last changes fastest.
Arguments:
- voltages: bfloat16 [512, 2, 55, 4096], P(('group', 'stn', 'tm'), 'pol'), parts along dimension 0, may hold values from -6 to 6
- fir_taps: bfloat16 [8, 2048], replicated, may hold values from -1.5 to 1.5
- owner_map: int32 [32, 1], replicated, may hold values from 0 to 7; in each aligned block of 32 rows (0 to 31, 32 to 63, ...) at most 8 rows name the same one
- station_flag_marks: int32 [256], P(('stn', 'tm')), may hold values 0 or 1
Outputs:
- visibilities: bfloat16 [16, 8, 2, 512, 512], P(('group', 'stn', 'tm'), None, None, 'pol'), parts along dimension 0
There are 2 independent parts, one for each index of `group`. A program takes and returns all parts, laid end to end along the dimension named above; an argument that names none is the same for every part. Nothing has to cross between parts.
Inputs may be any that keep to these rules, and one draw needn't show every extreme that they name: `owner_map`: no owner has more than 8 channels, some owner has exactly 8, and every owner has at least one.
All inputs are finite; a program needn't handle non-finite values. No bound on the sum of `station_flag_marks` on one device may be relied on, other than what follows from the above.
Results may differ from a plain program's by a relative error of at most 0.008.
Values may be sent and summed in bfloat16 or wider, within the bound.
A program may use at most 64 MiB of HBM per device.

v0:
```python
import math

import jax
import jax.numpy as jnp
from jax import lax
from jax.sharding import PartitionSpec as P


def partner(value, axis, stride):
    return lax.ppermute(value, axis, [(i, i ^ 1 << stride) for i in range(lax.axis_size(axis))])


def dft_table(fft_length, channels):
    row_numbers = jnp.arange(fft_length, dtype=jnp.int32)[:, None]
    col_ids = jnp.arange(channels, dtype=jnp.int32)[None, :]
    phase_idx = (row_numbers * col_ids % fft_length).astype(jnp.float32) * (
        2.0 * math.pi / fft_length
    )
    norm_scale = 1.0 / math.sqrt(fft_length)
    cosine = (jnp.cos(phase_idx) * norm_scale).astype(jnp.bfloat16)
    sine_part = (jnp.sin(phase_idx) * norm_scale).astype(jnp.bfloat16)
    upper_rows = jnp.concatenate([cosine, -sine_part], axis=1)
    lower_rows = jnp.concatenate([sine_part, cosine], axis=1)
    return jnp.concatenate([upper_rows, lower_rows], axis=0)


def slot_matches(route_map, owners, capacity):
    channels = route_map.shape[0]
    position = jnp.arange(channels, dtype=jnp.int32)
    earlier = (route_map[:, None] == route_map[None, :]) & (position[None, :] < position[:, None])
    position_within_owner = jnp.sum(earlier.astype(jnp.int32), axis=1)
    owner_ids = jnp.arange(owners, dtype=jnp.int32)
    slot_ids = jnp.arange(capacity, dtype=jnp.int32)
    return (route_map[None, None, :] == owner_ids[:, None, None]) & (
        position_within_owner[None, None, :] == slot_ids[None, :, None]
    )


def corner_turn(outgoing):
    return lax.all_to_all(outgoing, ("stn", "tm"), split_axis=3, concat_axis=3, tiled=True)


def body(voltages, fir_taps, owner_map, station_flag_marks):
    st_dev = voltages.shape[0]
    span_blocks = voltages.shape[2]
    fft_length = voltages.shape[3] // 2
    tap_count = fir_taps.shape[0]
    blocks = span_blocks - tap_count + 1
    channels = owner_map.shape[0]
    stn_count = lax.axis_size("stn")
    tm_count = lax.axis_size("tm")
    owners = stn_count * tm_count
    capacity = 2 * channels // owners
    stations = st_dev * owners
    pol_index = lax.axis_index("pol")
    table = dft_table(fft_length, channels)
    wide_taps = jnp.concatenate([fir_taps, fir_taps], axis=1).astype(jnp.float32)
    samples = voltages[:, 0]
    filtered = wide_taps[0] * samples[:, 0:blocks].astype(jnp.float32)
    for tap_index in range(1, tap_count):
        filtered = filtered + wide_taps[tap_index] * samples[
            :, tap_index : tap_index + blocks
        ].astype(jnp.float32)
    flat_rows = filtered.astype(jnp.bfloat16).reshape(st_dev * blocks, 2 * fft_length)
    single_spectrum = jnp.dot(flat_rows, table, preferred_element_type=jnp.float32).reshape(
        st_dev, blocks, 2, channels
    )
    clean_stations = (1 - station_flag_marks).astype(jnp.float32)
    channel_spectra = (single_spectrum * clean_stations[:, None, None, None]).astype(jnp.bfloat16)
    pick_matrix = slot_matches(owner_map[:, 0], owners, capacity).astype(jnp.bfloat16)
    outgoing = jnp.einsum(
        "okc,sbqc->kqosb", pick_matrix, channel_spectra, preferred_element_type=jnp.float32
    )
    outgoing = outgoing.astype(jnp.bfloat16).reshape(capacity, 2, 1, owners, st_dev * blocks)
    arrived = corner_turn(outgoing)
    row_block = arrived.reshape(capacity, 2, stations, blocks)
    other_block = partner(row_block, "pol", 0)
    col_block = jnp.where(
        pol_index == 0,
        jnp.concatenate([row_block, other_block], axis=2),
        jnp.concatenate([other_block, row_block], axis=2),
    )
    products = jnp.einsum(
        "kqib,krjb->kqrij", row_block, col_block, preferred_element_type=jnp.float32
    )
    real_part = (products[:, 0, 0] + products[:, 1, 1]) / blocks
    imag_part = (products[:, 1, 0] - products[:, 0, 1]) / blocks
    return jnp.stack([real_part, imag_part], axis=1).astype(jnp.bfloat16)[None]


def solution(mesh):
    in_specs = (P(("group", "stn", "tm"), "pol", None, None), P(), P(), P(("stn", "tm")))
    out_specs = P(("group", "stn", "tm"), None, None, "pol", None)
    return jax.shard_map(body, mesh=mesh, in_specs=in_specs, out_specs=out_specs, check_vma=False)
```

profile of v0, /device:TPU:0, one launch (start us, length us, event | category | flops | bytes accessed | tf_op | source)
XLA Modules:
  0.0 82.1 jit_solution(5008432259960567995)
XLA Ops:
  0.0 1.0 %fusion.31 = bf16[2048,32]{0,1:T(8,128)(2,1)S(1)} fusion(), kind=kLoop, calls=%fused_computation.42 | loop fusion | flops 1245184 | bytes 131072 | tf_op jit(solution)/shard_map/neg | solution.py:22
  1.0 1.1 %multiply_convert_fusion.1 = (bf16[2048,32]{0,1:T(8,128)(2,1)S(1)}, bf16[2048,32]{0,1:T(8,128)(2,1)S(1)}) fusion(), kind=kLoop, calls=%fused_computation.36 | loop fusion | flops 1179648 | bytes 262144 | tf_op jit(solution)/shard_map/convert_element_type | solution.py:21
  2.1 0.9 %convert_reduce_fusion = s32[32]{0:T(128)S(1)} fusion(s32[32]{0:T(128)} %bitcast.87), kind=kLoop, calls=%fused_computation.45 | loop fusion | flops 5088 | bytes 256 | tf_op jit(solution)/shard_map/reduce_sum | solution.py:31
  3.0 0.7 subtract_convert_fusion
  3.7 0.7 iota_compare_fusion.1
  4.3 0.8 %maximum_convert_fusion = f32[8,4096]{1,0:T(8,128)S(1)} fusion(bf16[8,2048]{1,0:T(8,128)(2,1)} %param.5), kind=kLoop, calls=%fused_computation.41 | loop fusion | flops 131072 | bytes 163840 | tf_op jit(solution)/shard_map/convert_element_type | solution.py:57
  5.2 0.1 fusion.38
  5.3 38.0 %fusion.12 = bf16[32,48,2,32,1]{3,0,2,1,4:T(8,128)(2,1)S(1)} fusion(bf16[2,32,4096,1]{2,1,0,3:T(8,128)(2,1)S(1)} %bitcast.78, bf16[32,55,4096]{2,0,1:T(8,128)(2,1)} %bitcast.89, f32[4096]{0:T(1024)S(1)} %bitcast.80, f32[4096]{0:T(1024)S(1)} %bitcast.81, f32[4096]{0:T(1024)S(1)} %bitcast.82, f32[4096]{0:T(1024)S(1)} %bitcast.83, f32[4096]{0:T(1024)S(1)} %bitcast.84, ...), kind=kOutput, calls=%fused_computation.18 | convolution fusion | flops 956497920 | bytes 101515392 | tf_op jit(solution)/shard_map/dot_general | solution.py:65
  43.3 1.1 %fusion.11 = bf16[8,2,8,32,48]{4,0,2,1,3:T(8,128)(2,1)S(1)} fusion(bf16[32,48,2,32,1]{3,0,2,1,4:T(8,128)(2,1)S(1)} %fusion.12, pred[8,32]{1,0:T(8,128)(4,1)S(1)} %get-tuple-element.15, pred[8,32]{1,0:T(8,128)(4,1)S(1)} %get-tuple-element.16), kind=kOutput, calls=%fused_computation.17 | convolution fusion | flops 12781568 | bytes 590336 | tf_op jit(solution)/shard_map/okc,sbqc->kqosb/dot_general | solution.py:71
  44.4 0.7 copy.47
  45.1 1.7 %reshape.169 = bf16[8,2,1,8,1536]{4,1,0,2,3:T(2,128)(2,1)S(1)} reshape(bf16[8,2,8,32,48]{4,3,1,0,2:T(8,128)(2,1)S(1)} %copy.47) | data formatting | bytes 786432 | tf_op jit(solution)/shard_map/reshape | solution.py:74
  46.8 19.2 %all_to_all.5 = bf16[8,2,1,8,1536]{4,1,0,2,3:T(2,128)(2,1)S(1)} all-to-all(bf16[8,2,1,8,1536]{4,1,0,2,3:T(2,128)(2,1)S(1)} %reshape.169), channel_id=1, replica_groups=mesh['group'=2,'stn'=4,'tm'=2,'pol'=2] {'stn','tm'}, dimensions={3} | all-to-all | bytes 786432 | tf_op jit(solution)/shard_map/all_to_all | solution.py:40
  66.0 0.2 copy.31
  66.2 1.1 %reshape.162 = bf16[8,2,256,48]{3,2,1,0:T(8,128)(2,1)S(1)} reshape(bf16[8,2,1,8,1536]{4,3,1,0,2:T(8,128)(2,1)S(1)} %copy.31) | data formatting | bytes 786432 | tf_op jit(solution)/shard_map/reshape | solution.py:76
  67.2 0.4 copy.33
  67.6 0.1 collective-permute-start
  67.7 1.7 %collective-permute-done = bf16[8,2,256,48]{2,3,1,0:T(8,128)(2,1)S(1)} collective-permute-done((bf16[8,2,256,48]{2,3,1,0:T(8,128)(2,1)S(1)}, bf16[8,2,256,48]{2,3,1,0:T(8,128)(2,1)S(1)}, u32[]{:S(2)}, u32[]{:S(2)}) %collective-permute-start) | collective-permute-done | bytes 393248 | tf_op jit(solution)/shard_map/ppermute | solution.py:10
  69.4 2.4 %convolution_bitcast_fusion = f32[8,2,2,256,512]{3,4,1,2,0:T(8,128)S(1)} fusion(bf16[8,2,256,48]{3,2,1,0:T(8,128)(2,1)S(1)} %reshape.162, bf16[8,2,256,48]{2,3,1,0:T(8,128)(2,1)S(1)} %collective-permute-done, bf16[8,2,256,48]{2,3,1,0:T(8,128)(2,1)S(1)} %copy.33, pred[]{:T(512)S(6)} %eq.56), kind=kOutput, calls=%fused_computation.3 | convolution fusion | flops 406192128 | bytes 17956864 | tf_op jit(solution)/shard_map/kqib,krjb->kqrij/dot_general | solution.py:83
  71.8 0.8 fusion.8
  72.6 0.8 fusion.7
  73.4 2.3 %pad_maximum_fusion = bf16[1,8,2,256,512]{3,4,1,2,0:T(8,128)(2,1)} fusion(bf16[1,8,1,256,512]{3,4,1,2,0:T(8,128)(2,1)S(1)} %fusion.8, bf16[1,8,1,256,512]{3,4,1,2,0:T(8,128)(2,1)S(1)} %fusion.7), kind=kLoop, calls=%fused_computation.12 | loop fusion | flops 2097152 | bytes 8388608 | tf_op jit(solution)/shard_map/stack | solution.py:88
  75.7 6.4 %copy.39 = bf16[1,8,2,256,512]{4,3,2,1,0:T(8,128)(2,1)} copy(bf16[1,8,2,256,512]{3,4,1,2,0:T(8,128)(2,1)} %pad_maximum_fusion) | data formatting | bytes 8388608 | tf_op jit(solution)/shard_map/stack | solution.py:88
  (1 shorter events, 0.0 us)
Async XLA Ops:
  67.6 1.8 %collective-permute-start = (bf16[8,2,256,48]{2,3,1,0:T(8,128)(2,1)S(1)}, bf16[8,2,256,48]{2,3,1,0:T(8,128)(2,1)S(1)}, u32[]{:S(2)}, u32[]{:S(2)}) collective-permute-start(bf16[8,2,256,48]{2,3,1,0:T(8,128)(2,1)S(1)} %copy.33), channel_id=1, source_target_pairs={{0,1},{1,0},{2,3},{3,2},{4,5},{5,4},{6,7},{7,6},{8,9},{9,8},{10,11... | collective-permute-start | bytes 1179656 | tf_op jit(solution)/shard_map/ppermute | solution.py:10
where the time goes:
time: 82.5 us; the launch traced here: 82.1 us
  matrix products  41.4 us (50%)
  blocking collectives  19.2 us (23%)
  local copies, waits for them, and re-layouts  10.6 us (13%)
  other arithmetic  9.04 us (11%)
  waiting for transfers between devices  1.7 us (2%)
    dot_general x1, matrix products, body(): jnp.dot(flat_rows, table, preferred_element_type=jnp.float32)  38 us
    all_to_all x1, blocking collectives, corner_turn(): lax.all_to_all(outgoing, ('stn', 'tm'), split_axis=3, concat_axis=3, tile...  19.2 us
    another operation x1, local copies, waits for them, and re-layouts, body(): return jnp.stack([real_part, imag_part], axis=1).astype(jnp.bfloat16)[None]  6.44 us
    another operation x3, other arithmetic, body(): return jnp.stack([real_part, imag_part], axis=1).astype(jnp.bfloat16)[None]  3.86 us
    reshape x2, local copies, waits for them, and re-layouts, body(): outgoing.astype(jnp.bfloat16)  2.42 us
    dot_general x1, matrix products, body(): jnp.einsum('kqib,krjb->kqrij', row_block, col_block, preferred_element_ty...  2.38 us
    ppermute x1, waiting for transfers between devices, partner(): lax.ppermute(value, axis, [(i, i ^ 1 << stride) for i in range(lax.axis_s...  1.7 us
  transfers between devices with their start and end apart: 1, of which 1 were waited for; matrix products, arithmetic and copies ran while one was open for 0% of the time, Pallas kernels for 0%

commit v1 on v0

--- a/solution.py
+++ b/solution.py
@@ -1,8 +1,12 @@
+import functools
 import math
 
 import jax
 import jax.numpy as jnp
+import numpy as np
 from jax import lax
+from jax.experimental import pallas as pl
+from jax.experimental.pallas import tpu as pltpu
 from jax.sharding import PartitionSpec as P
 
 
@@ -40,7 +44,7 @@
     return lax.all_to_all(outgoing, ("stn", "tm"), split_axis=3, concat_axis=3, tiled=True)
 
 
-def body(voltages, fir_taps, owner_map, station_flag_marks):
+def general_body(voltages, fir_taps, owner_map, station_flag_marks):
     st_dev = voltages.shape[0]
     span_blocks = voltages.shape[2]
     fft_length = voltages.shape[3] // 2
@@ -88,6 +92,306 @@
     return jnp.stack([real_part, imag_part], axis=1).astype(jnp.bfloat16)[None]
 
 
+GROUP = 8
+STEP = 16
+LANES = 128
+
+
+def wide_table(fft_length, channels):
+    n = np.arange(fft_length, dtype=np.int64)[:, None]
+    k = np.arange(channels, dtype=np.int64)[None, :]
+    phase = (n * k % fft_length).astype(np.float32) * np.float32(2.0 * math.pi / fft_length)
+    scale = np.float32(1.0 / math.sqrt(fft_length))
+    cosine = (np.cos(phase) * scale).astype(jnp.bfloat16)
+    sine = (np.sin(phase) * scale).astype(jnp.bfloat16)
+    upper = np.concatenate([cosine, -sine], axis=1)
+    lower = np.concatenate([sine, cosine], axis=1)
+    whole = np.concatenate([upper, lower], axis=0)
+    return np.concatenate([whole] * (LANES // (2 * channels)), axis=1)
+
+
+def iota(shape, dim):
+    return lax.broadcasted_iota(jnp.int32, shape, dim)
+
+
+def slot_columns(owner_ref, channels, capacity):
+    col = owner_ref[...]
+    lane = iota((channels, LANES), 1)
+    channel = lane % channels
+    row_number = iota((channels, LANES), 0)
+    owner = jnp.sum(jnp.where(row_number == channel, col, 0), axis=0, keepdims=True)
+    rank = jnp.sum(
+        jnp.where((col == owner) & (row_number < channel), 1, 0), axis=0, keepdims=True
+    )
+    lane = iota((1, LANES), 1)
+    place = (owner * capacity + rank) * 2 + lane // channels
+    place = jnp.where(lane < 2 * channels, place, -1)
+    hot = jnp.where(iota((LANES, LANES), 0) == place, 1.0, 0.0)
+    return hot.T.astype(jnp.bfloat16)
+
+
+def block_transpose(parts, width):
+    count = len(parts)
+    lane = iota(parts[0].shape, 1) // width
+    half = 1
+    while half < count:
+        low = lane // half % 2 == 0
+        out = list(parts)
+        for i in range(count):
+            if i // half % 2 == 0:
+                a, b = parts[i], parts[i + half]
+                out[i] = jnp.where(low, a, pltpu.roll(b, half * width, 1))
+                out[i + half] = jnp.where(low, pltpu.roll(a, LANES - half * width, 1), b)
+        parts = out
+        half *= 2
+    return parts
+
+
+def channelize_kernel(
+    sizes, v_ref, taps_ref, table_ref, owner_ref, marks_ref, x_ref,
+    vbuf, tail, wbuf, zbuf, sendbuf, in_sem, send_sem, recv_sem, own_sem, pass_send, pass_recv,
+):
+    stations, span, samples, taps, blocks, channels, owners, capacity, tm_count = sizes
+    steps = -(-span // STEP)
+    groups = blocks // GROUP
+    width = 2 * capacity
+    pol = lax.axis_index("pol")
+    me = lax.axis_index("stn") * tm_count + lax.axis_index("tm")
+
+    loads = []
+    for c in range(steps):
+        rows = min(STEP, span - c * STEP)
+        load = pltpu.make_async_copy(
+            v_ref.at[:, 0, pl.ds(c * STEP, rows), :],
+            vbuf.at[c] if rows == STEP else tail,
+            in_sem.at[c],
+        )
+        load.start()
+        loads.append(load)
+
+    barrier = pltpu.get_barrier_semaphore()
+    for k in range(1, owners):
+        peer = lax.rem(me + k, owners)
+        pl.semaphore_signal(
+            barrier, inc=1, device_id={"stn": peer // tm_count, "tm": lax.rem(peer, tm_count)},
+            device_id_type=pl.DeviceIdType.MESH,
+        )
+    pl.semaphore_signal(
+        barrier, inc=1, device_id={"pol": 1 - pol}, device_id_type=pl.DeviceIdType.MESH
+    )
+
+    columns = taps * 2 * channels
+    expand = jnp.where(
+        iota((taps, columns), 0) == iota((taps, columns), 1) // (2 * channels), 1.0, 0.0
+    ).astype(jnp.bfloat16)
+    half = samples // 2
+    piece = 256
+    for i in range(half // piece):
+        tap_rows = lax.dot_general(
+            taps_ref[:, i * piece : (i + 1) * piece], expand,
+            (((0,), (0,)), ((), ())), preferred_element_type=jnp.float32,
+        )
+        for base in (0, half):
+            at = slice(base + i * piece, base + (i + 1) * piece)
+            entry = table_ref[at, :].astype(jnp.float32)
+            for j in range(columns // LANES):
+                lanes = slice(j * LANES, (j + 1) * LANES)
+                wbuf[at, lanes] = (tap_rows[:, lanes] * entry).astype(jnp.bfloat16)
+
+    pick = slot_columns(owner_ref, channels, capacity)
+    diagonal = iota((stations, stations), 0) == iota((stations, stations), 1)
+    keep = 1.0 - jnp.sum(
+        jnp.where(diagonal, marks_ref[...], 0), axis=1, keepdims=True
+    ).astype(jnp.float32)
+    pl.semaphore_wait(barrier, owners)
+
+    def shifted(b):
+        total = None
+        for j in range(columns // LANES):
+            row = b + 2 * j
+            first = row // STEP * stations * STEP + row % STEP
+            term = zbuf[j, pl.ds(first, stations, stride=STEP), :]
+            total = term if total is None else total + term
+        return total
+
+    sends, passes = [], []
+
+    def send_groups(c, first, last):
+        lanes = pl.ds(first * LANES, (last - first) * LANES)
+        rows = pl.ds(me * stations, stations)
+        for g in range(first, last):
+            summed = [shifted(g * GROUP + i) for i in range(GROUP + 1)]
+            spectra = [
+                ((summed[i] + pltpu.roll(summed[i + 1], 2 * channels, 1)) * keep).astype(jnp.bfloat16)
+                for i in range(GROUP)
+            ]
+            placed = jnp.dot(
+                jnp.concatenate(spectra, axis=0), pick, preferred_element_type=jnp.float32
+            )
+            parts = [placed[i * stations : (i + 1) * stations] for i in range(GROUP)]
+            for o, part in enumerate(block_transpose(parts, width)):
+                sendbuf[o, :, g * LANES : (g + 1) * LANES] = part.astype(jnp.bfloat16)
+        batch = []
+        for k in range(1, owners):
+            peer = lax.rem(me + k, owners)
+            copy = pltpu.make_async_remote_copy(
+                src_ref=sendbuf.at[peer, :, lanes],
+                dst_ref=x_ref.at[pol, rows, lanes],
+                send_sem=send_sem.at[c, k],
+                recv_sem=recv_sem.at[c, k],
+                device_id={"stn": peer // tm_count, "tm": lax.rem(peer, tm_count)},
+                device_id_type=pl.DeviceIdType.MESH,
+            )
+            copy.start()
+            batch.append(copy)
+        own = pltpu.make_async_copy(
+            sendbuf.at[me, :, lanes], x_ref.at[pol, rows, lanes], own_sem.at[c]
+        )
+        own.start()
+        sends.append((batch, own, lanes))
+
+    def pass_on(c):
+        batch, own, lanes = sends[c]
+        own.wait()
+        for k in range(1, owners):
+            source = lax.rem(me + owners - k, owners)
+            here = x_ref.at[pol, pl.ds(source * stations, stations), lanes]
+            pltpu.make_async_copy(here, here, recv_sem.at[c, k]).wait()
+        mine = x_ref.at[pol, :, lanes]
+        copy = pltpu.make_async_remote_copy(
+            src_ref=mine, dst_ref=mine, send_sem=pass_send.at[c], recv_sem=pass_recv.at[c],
+            device_id={"pol": 1 - pol}, device_id_type=pl.DeviceIdType.MESH,
+        )
+        copy.start()
+        passes.append(copy)
+
+    done = 0
+    for c in range(steps):
+        loads[c].wait()
+        if span - c * STEP < STEP:
+            vbuf[c, :, 0 : tail.shape[1], :] = tail[...]
+        product = jnp.dot(
+            vbuf[c].reshape(stations * STEP, samples), wbuf[...],
+            preferred_element_type=jnp.float32,
+        )
+        for j in range(columns // LANES):
+            zbuf[j, c * stations * STEP : (c + 1) * stations * STEP, :] = product[
+                :, j * LANES : (j + 1) * LANES
+            ]
+        if c >= 1:
+            pass_on(c - 1)
+        ready = min(groups, (min(span, (c + 1) * STEP) - taps + 1) // GROUP)
+        send_groups(c, done, ready)
+        done = ready
+    pass_on(steps - 1)
+    for batch, own, lanes in sends:
+        for copy in batch:
+            copy.wait_send()
+    for copy in passes:
+        copy.wait()
+
+
+def correlate_kernel(blocks, capacity, x_ref, out_ref, held):
+    k = pl.program_id(0)
+    pol = lax.axis_index("pol")
+    rows, depth = x_ref.shape[1], x_ref.shape[2]
+    lane = iota((1, 2 * LANES), 1)
+    swapped = lane // LANES
+    inner = lane % LANES
+    part = inner // blocks
+    wanted = inner % blocks * (2 * capacity) + 2 * k + jnp.where(swapped == 1, 1 - part, part)
+    wanted = jnp.where(inner < 2 * blocks, wanted, -1)
+    sign = jnp.where((swapped == 1) & (part == 1), -1.0, 1.0)
+    place = jnp.where(iota((depth, 2 * LANES), 0) == wanted, sign, 0.0).astype(jnp.bfloat16)
+    held[...] = (
+        jnp.dot(x_ref[...].reshape(2 * rows, depth), place, preferred_element_type=jnp.float32)
+        .astype(jnp.bfloat16)
+        .reshape(2, rows, 2 * LANES)
+    )
+    right = held[:, :, 0:LANES].reshape(2 * rows, LANES)
+    for q in range(2):
+        product = lax.dot_general(
+            held[pol, :, q * LANES : (q + 1) * LANES], right, (((1,), (1,)), ((), ())),
+            preferred_element_type=jnp.float32,
+        )
+        out_ref[0, 0, q] = (product * (1.0 / blocks)).astype(jnp.bfloat16)
+
+
+def fast_body(voltages, fir_taps, owner_map, station_flag_marks):
+    stations, _, span, samples = voltages.shape
+    taps = fir_taps.shape[0]
+    blocks = span - taps + 1
+    channels = owner_map.shape[0]
+    tm_count = lax.axis_size("tm")
+    owners = lax.axis_size("stn") * tm_count
+    capacity = 2 * channels // owners
+    steps = -(-span // STEP)
+    lanes = blocks * 2 * capacity
+    columns = taps * 2 * channels
+    sizes = (stations, span, samples, taps, blocks, channels, owners, capacity, tm_count)
+    vmem = pl.BlockSpec(memory_space=pltpu.VMEM)
+    dma = pltpu.SemaphoreType.DMA
+    x = pl.pallas_call(
+        functools.partial(channelize_kernel, sizes),
+        out_shape=jax.ShapeDtypeStruct((2, owners * stations, lanes), jnp.bfloat16),
+        in_specs=[pl.BlockSpec(memory_space=pl.ANY), vmem, vmem, vmem, vmem],
+        out_specs=vmem,
+        scratch_shapes=[
+            pltpu.VMEM((steps, stations, STEP, samples), jnp.bfloat16),
+            pltpu.VMEM((stations, (span - 1) % STEP + 1, samples), jnp.bfloat16),
+            pltpu.VMEM((samples, columns), jnp.bfloat16),
+            pltpu.VMEM((columns // LANES, steps * stations * STEP, LANES), jnp.float32),
+            pltpu.VMEM((owners, stations, lanes), jnp.bfloat16),
+            dma((steps,)),
+            dma((steps, owners)),
+            dma((steps, owners)),
+            dma((steps,)),
+            dma((steps,)),
+            dma((steps,)),
+        ],
+        compiler_params=pltpu.CompilerParams(
+            collective_id=0, has_side_effects=True, vmem_limit_bytes=48 * 1024 * 1024
+        ),
+        name="channelize",
+    )(
+        voltages, fir_taps, jnp.asarray(wide_table(samples // 2, channels)), owner_map,
+        station_flag_marks.reshape(1, stations),
+    )
+    rows = owners * stations
+    return pl.pallas_call(
+        functools.partial(correlate_kernel, blocks, capacity),
+        grid=(capacity,),
+        out_shape=jax.ShapeDtypeStruct((1, capacity, 2, rows, 2 * rows), jnp.bfloat16),
+        in_specs=[pl.BlockSpec((2, rows, lanes), lambda k: (0, 0, 0))],
+        out_specs=pl.BlockSpec((1, 1, 2, rows, 2 * rows), lambda k: (0, k, 0, 0, 0)),
+        scratch_shapes=[pltpu.VMEM((2, rows, 2 * LANES), jnp.bfloat16)],
+        compiler_params=pltpu.CompilerParams(vmem_limit_bytes=32 * 1024 * 1024),
+        name="correlate",
+    )(x)
+
+
+def body(voltages, fir_taps, owner_map, station_flag_marks):
+    stations, _, span, samples = voltages.shape
+    taps = fir_taps.shape[0]
+    channels = owner_map.shape[0]
+    blocks = span - taps + 1
+    owners = lax.axis_size("stn") * lax.axis_size("tm")
+    width = 4 * channels // owners
+    fits = (
+        4 * channels == LANES
+        and owners * width == LANES
+        and GROUP * width == LANES
+        and taps == GROUP
+        and blocks % GROUP == 0
+        and 2 * blocks <= LANES
+        and stations % 16 == 0
+        and samples % 512 == 0
+        and lax.axis_size("pol") == 2
+    )
+    run = fast_body if fits else general_body
+    return run(voltages, fir_taps, owner_map, station_flag_marks)
+
+
 def solution(mesh):
     in_specs = (P(("group", "stn", "tm"), "pol", None, None), P(), P(), P(("stn", "tm")))
     out_specs = P(("group", "stn", "tm"), None, None, "pol", None)

time: 82.5 us -> 55.4 us (0.67)
  matrix products: 41.4 us -> 0 us
  Pallas kernels: 0 us -> 37.7 us
  blocking collectives: 19.2 us -> 0 us
  other arithmetic: 9.04 us -> 0 us
  local copies, waits for them, and re-layouts: 10.6 us -> 17.3 us
  waiting for transfers between devices: 1.7 us -> 0 us
    dot_general x3 -> x0, matrix products: 41.4 us -> none  [the longest x1 38 us: body(): jnp.dot(flat_rows, table, preferred_element_type=jnp.float32)]
    pallas_call x0 -> x2, Pallas kernels: none -> 37.7 us  [the longest x1 30 us: fast_body(): pl.pallas_call(functools.partial(channelize_kernel, sizes), out_shape=jax...]
    all_to_all x1 -> x0, blocking collectives: 19.2 us -> none  [corner_turn(): lax.all_to_all(outgoing, ('stn', 'tm'), split_axis=3, concat_axis=3, tile...]
    unnamed x0 -> x8, local copies, waits for them, and re-layouts: none -> 17.3 us
    another operation x1 -> x0, local copies, waits for them, and re-layouts: 6.44 us -> none  [body(): return jnp.stack([real_part, imag_part], axis=1).astype(jnp.bfloat16)[None]]
    another operation x3 -> x0, other arithmetic: 3.86 us -> none  [body(): return jnp.stack([real_part, imag_part], axis=1).astype(jnp.bfloat16)[None]]
    reshape x4 -> x0, local copies, waits for them, and re-layouts: 3.83 us -> none  [the longest x2 2.42 us: body(): outgoing.astype(jnp.bfloat16)]
    convert_element_type x3 -> x0, other arithmetic: 2.6 us -> none  [the longest x1 1.09 us: dft_table(): sine_part = (jnp.sin(phase_idx) * norm_scale).astype(jnp.bfloat16)]
  transfers between devices with their start and end apart: 1 -> 0, of which waited for: 1 -> 0; matrix products, arithmetic and copies ran while one was open for 0% -> 0% of each run, Pallas kernels for 0% -> 0%
where the time goes in v1:
time: 55.4 us; the launch traced here: 55 us
  Pallas kernels  37.7 us (68%)
  local copies, waits for them, and re-layouts  17.3 us (31%)
    pallas_call x1, Pallas kernels, fast_body(): pl.pallas_call(functools.partial(channelize_kernel, sizes), out_shape=jax...  30 us
    unnamed x8, local copies, waits for them, and re-layouts  17.3 us
    pallas_call x1, Pallas kernels, fast_body(): pl.pallas_call(functools.partial(correlate_kernel, blocks, capacity), gri...  7.73 us

profile of v1, /device:TPU:0, one launch (start us, length us, event | category | flops | bytes accessed | tf_op | source)
XLA Modules:
  0.0 55.0 jit_solution(5117325400216187405)
XLA Ops:
  0.0 0.7 %copy.7.owner_ref = s32[32,1]{1,0:T(8,128)S(1)} copy(s32[32,1]{0,1:T(1,128)} %param.7) | data formatting | bytes 256 | tf_op args[2]
  0.7 0.0 copy-start
  0.7 0.0 copy-start.1
  0.7 0.0 copy-start.2
  0.7 16.6 %copy.6.v_ref = bf16[32,1,55,4096]{3,2,1,0:T(8,128)(2,1)} copy(bf16[32,1,55,4096]{3,0,2,1:T(8,128)(2,1)} %param.5) | data formatting | bytes 28835840 | tf_op args[0]
  17.3 0.0 copy-done
  17.3 0.0 copy-done.1
  17.3 0.0 copy-done.2
  17.4 30.0 %channelize.1.x_ref = bf16[2,256,768]{2,1,0:T(8,128)(2,1)S(1)} custom-call(bf16[32,1,55,4096]{3,2,1,0:T(8,128)(2,1)} %copy.6.v_ref, bf16[8,2048]{1,0:T(8,128)(2,1)S(1)} %copy-done.1, bf16[4096,128]{1,0:T(8,128)(2,1)S(1)} %copy-done, s32[32,1]{1,0:T(8,128)S(1)} %copy.7.owner_ref, s32[1,32]{1,0:T(1,128)S(1)} %bitcast.1), custom_call_target="tpu_custom_call" | custom-call | tf_op jit(solution)/shard_map/channelize/pallas_call | solution.py:334
  47.3 7.7 %correlate.1 = bf16[1,8,2,256,512]{4,3,2,1,0:T(8,128)(2,1)} custom-call(bf16[2,256,768]{2,1,0:T(8,128)(2,1)S(1)} %channelize.1.x_ref), custom_call_target="tpu_custom_call" | custom-call | tf_op jit(solution)/shard_map/correlate/pallas_call | solution.py:361
Async XLA Ops:
  0.7 16.6 %copy-start = (bf16[4096,128]{1,0:T(8,128)(2,1)S(1)}, bf16[4096,128]{1,0:T(8,128)(2,1)}, u32[]{:S(2)}) copy-start(bf16[4096,128]{1,0:T(8,128)(2,1)} %constant.2.clone.table_ref) | copy-start | bytes 3145732
  0.7 16.6 %copy-start.1 = (bf16[8,2048]{1,0:T(8,128)(2,1)S(1)}, bf16[8,2048]{1,0:T(8,128)(2,1)}, u32[]{:S(2)}) copy-start(bf16[8,2048]{1,0:T(8,128)(2,1)} %taps_ref.1) | copy-start | bytes 98308
  0.7 16.6 %copy-start.2 = (s32[32]{0:T(128)S(1)}, s32[32]{0:T(128)}, u32[]{:S(2)}) copy-start(s32[32]{0:T(128)} %param.8) | copy-start | bytes 388

commit v2 on v1

--- a/solution.py
+++ b/solution.py
@@ -93,7 +93,6 @@
 
 
 GROUP = 8
-STEP = 16
 LANES = 128
 
 
@@ -110,12 +109,17 @@
     return np.concatenate([whole] * (LANES // (2 * channels)), axis=1)
 
 
+def row_cuts(groups):
+    return [0] + list(range(1, groups, 2)) + [groups]
+
+
 def iota(shape, dim):
     return lax.broadcasted_iota(jnp.int32, shape, dim)
 
 
 def slot_columns(owner_ref, channels, capacity):
-    col = owner_ref[...]
+    square = iota((channels, channels), 0) == iota((channels, channels), 1)
+    col = jnp.sum(jnp.where(square, owner_ref[...], 0), axis=1, keepdims=True)
     lane = iota((channels, LANES), 1)
     channel = lane % channels
     row_number = iota((channels, LANES), 0)
@@ -149,23 +153,20 @@
 
 def channelize_kernel(
     sizes, v_ref, taps_ref, table_ref, owner_ref, marks_ref, x_ref,
-    vbuf, tail, wbuf, zbuf, sendbuf, in_sem, send_sem, recv_sem, own_sem, pass_send, pass_recv,
+    vbuf, wbuf, zbuf, sendbuf, in_sem, send_sem, recv_sem, own_sem, pass_send, pass_recv,
 ):
     stations, span, samples, taps, blocks, channels, owners, capacity, tm_count = sizes
-    steps = -(-span // STEP)
-    groups = blocks // GROUP
+    cuts = row_cuts(blocks // GROUP)
+    steps = len(cuts) - 1
     width = 2 * capacity
     pol = lax.axis_index("pol")
     me = lax.axis_index("stn") * tm_count + lax.axis_index("tm")
+    ends = [0] + [cut * GROUP + taps - 1 for cut in cuts[1:]]
 
     loads = []
     for c in range(steps):
-        rows = min(STEP, span - c * STEP)
-        load = pltpu.make_async_copy(
-            v_ref.at[:, 0, pl.ds(c * STEP, rows), :],
-            vbuf.at[c] if rows == STEP else tail,
-            in_sem.at[c],
-        )
+        rows = pl.ds(ends[c], ends[c + 1] - ends[c])
+        load = pltpu.make_async_copy(v_ref.at[rows], vbuf.at[rows], in_sem.at[c])
         load.start()
         loads.append(load)
 
@@ -209,8 +210,7 @@
         total = None
         for j in range(columns // LANES):
             row = b + 2 * j
-            first = row // STEP * stations * STEP + row % STEP
-            term = zbuf[j, pl.ds(first, stations, stride=STEP), :]
+            term = zbuf[row * stations : (row + 1) * stations, j * LANES : (j + 1) * LANES]
             total = term if total is None else total + term
         return total
 
@@ -265,24 +265,16 @@
         copy.start()
         passes.append(copy)
 
-    done = 0
     for c in range(steps):
         loads[c].wait()
-        if span - c * STEP < STEP:
-            vbuf[c, :, 0 : tail.shape[1], :] = tail[...]
-        product = jnp.dot(
-            vbuf[c].reshape(stations * STEP, samples), wbuf[...],
+        first, last = ends[c], ends[c + 1]
+        zbuf[first * stations : last * stations, :] = jnp.dot(
+            vbuf[first:last].reshape((last - first) * stations, samples), wbuf[...],
             preferred_element_type=jnp.float32,
         )
-        for j in range(columns // LANES):
-            zbuf[j, c * stations * STEP : (c + 1) * stations * STEP, :] = product[
-                :, j * LANES : (j + 1) * LANES
-            ]
         if c >= 1:
             pass_on(c - 1)
-        ready = min(groups, (min(span, (c + 1) * STEP) - taps + 1) // GROUP)
-        send_groups(c, done, ready)
-        done = ready
+        send_groups(c, cuts[c], cuts[c + 1])
     pass_on(steps - 1)
     for batch, own, lanes in sends:
         for copy in batch:
@@ -291,30 +283,42 @@
         copy.wait()
 
 
-def correlate_kernel(blocks, capacity, x_ref, out_ref, held):
-    k = pl.program_id(0)
+def lane_places(blocks, capacity):
+    table = np.zeros((blocks, capacity, 2, capacity, 2, LANES // 2), np.float32)
+    for k in range(capacity):
+        for q in range(2):
+            table[np.arange(blocks), k, q, k, q, np.arange(blocks)] = 1.0
+    return table.reshape(blocks * capacity * 2, capacity * LANES).astype(jnp.bfloat16)
+
+
+def correlate_kernel(blocks, capacity, x_ref, place_ref, out_ref, held, result, out_sem):
     pol = lax.axis_index("pol")
     rows, depth = x_ref.shape[1], x_ref.shape[2]
-    lane = iota((1, 2 * LANES), 1)
-    swapped = lane // LANES
-    inner = lane % LANES
-    part = inner // blocks
-    wanted = inner % blocks * (2 * capacity) + 2 * k + jnp.where(swapped == 1, 1 - part, part)
-    wanted = jnp.where(inner < 2 * blocks, wanted, -1)
-    sign = jnp.where((swapped == 1) & (part == 1), -1.0, 1.0)
-    place = jnp.where(iota((depth, 2 * LANES), 0) == wanted, sign, 0.0).astype(jnp.bfloat16)
-    held[...] = (
-        jnp.dot(x_ref[...].reshape(2 * rows, depth), place, preferred_element_type=jnp.float32)
-        .astype(jnp.bfloat16)
-        .reshape(2, rows, 2 * LANES)
-    )
-    right = held[:, :, 0:LANES].reshape(2 * rows, LANES)
-    for q in range(2):
-        product = lax.dot_general(
-            held[pol, :, q * LANES : (q + 1) * LANES], right, (((1,), (1,)), ((), ())),
-            preferred_element_type=jnp.float32,
-        )
-        out_ref[0, 0, q] = (product * (1.0 / blocks)).astype(jnp.bfloat16)
+    signal = x_ref[...].reshape(2 * rows, depth)
+    sign = jnp.where(iota((1, LANES), 1) < LANES // 2, 1.0, -1.0)
+    copies = []
+    for pair in range(capacity // 2):
+        lanes = slice(pair * 2 * LANES, (pair + 1) * 2 * LANES)
+        held[:, :, lanes] = (
+            jnp.dot(signal, place_ref[:, lanes], preferred_element_type=jnp.float32)
+            .astype(jnp.bfloat16)
+            .reshape(2, rows, 2 * LANES)
+        )
+        for k in (2 * pair, 2 * pair + 1):
+            lanes = slice(k * LANES, (k + 1) * LANES)
+            right = held[:, :, lanes].reshape(2 * rows, LANES)
+            left = held[pol, :, lanes]
+            turned = pltpu.roll(left.astype(jnp.float32), LANES // 2, 1) * sign
+            for q, operand in enumerate((left, turned.astype(jnp.bfloat16))):
+                product = lax.dot_general(
+                    operand, right, (((1,), (1,)), ((), ())), preferred_element_type=jnp.float32
+                )
+                result[k, q] = (product * (1.0 / blocks)).astype(jnp.bfloat16)
+            copy = pltpu.make_async_copy(result.at[k], out_ref.at[0, k], out_sem.at[k])
+            copy.start()
+            copies.append(copy)
+    for copy in copies:
+        copy.wait()
 
 
 def fast_body(voltages, fir_taps, owner_map, station_flag_marks):
@@ -325,7 +329,7 @@
     tm_count = lax.axis_size("tm")
     owners = lax.axis_size("stn") * tm_count
     capacity = 2 * channels // owners
-    steps = -(-span // STEP)
+    steps = len(row_cuts(blocks // GROUP)) - 1
     lanes = blocks * 2 * capacity
     columns = taps * 2 * channels
     sizes = (stations, span, samples, taps, blocks, channels, owners, capacity, tm_count)
@@ -337,10 +341,9 @@
         in_specs=[pl.BlockSpec(memory_space=pl.ANY), vmem, vmem, vmem, vmem],
         out_specs=vmem,
         scratch_shapes=[
-            pltpu.VMEM((steps, stations, STEP, samples), jnp.bfloat16),
-            pltpu.VMEM((stations, (span - 1) % STEP + 1, samples), jnp.bfloat16),
+            pltpu.VMEM((span, stations, samples), jnp.bfloat16),
             pltpu.VMEM((samples, columns), jnp.bfloat16),
-            pltpu.VMEM((columns // LANES, steps * stations * STEP, LANES), jnp.float32),
+            pltpu.VMEM((span * stations, columns), jnp.float32),
             pltpu.VMEM((owners, stations, lanes), jnp.bfloat16),
             dma((steps,)),
             dma((steps, owners)),
@@ -350,24 +353,28 @@
             dma((steps,)),
         ],
         compiler_params=pltpu.CompilerParams(
-            collective_id=0, has_side_effects=True, vmem_limit_bytes=48 * 1024 * 1024
+            collective_id=0, has_side_effects=True, vmem_limit_bytes=52 * 1024 * 1024
         ),
         name="channelize",
     )(
-        voltages, fir_taps, jnp.asarray(wide_table(samples // 2, channels)), owner_map,
+        jnp.transpose(voltages[:, 0], (1, 0, 2)), fir_taps, jnp.asarray(wide_table(samples // 2, channels)),
+        owner_map.reshape(1, channels),
         station_flag_marks.reshape(1, stations),
     )
     rows = owners * stations
     return pl.pallas_call(
         functools.partial(correlate_kernel, blocks, capacity),
-        grid=(capacity,),
         out_shape=jax.ShapeDtypeStruct((1, capacity, 2, rows, 2 * rows), jnp.bfloat16),
-        in_specs=[pl.BlockSpec((2, rows, lanes), lambda k: (0, 0, 0))],
-        out_specs=pl.BlockSpec((1, 1, 2, rows, 2 * rows), lambda k: (0, k, 0, 0, 0)),
-        scratch_shapes=[pltpu.VMEM((2, rows, 2 * LANES), jnp.bfloat16)],
-        compiler_params=pltpu.CompilerParams(vmem_limit_bytes=32 * 1024 * 1024),
+        in_specs=[vmem, vmem],
+        out_specs=pl.BlockSpec(memory_space=pl.ANY),
+        scratch_shapes=[
+            pltpu.VMEM((2, rows, capacity * LANES), jnp.bfloat16),
+            pltpu.VMEM((capacity, 2, rows, 2 * rows), jnp.bfloat16),
+            dma((capacity,)),
+        ],
+        compiler_params=pltpu.CompilerParams(vmem_limit_bytes=24 * 1024 * 1024),
         name="correlate",
-    )(x)
+    )(x, jnp.asarray(lane_places(blocks, capacity)))
 
 
 def body(voltages, fir_taps, owner_map, station_flag_marks):
@@ -383,7 +390,8 @@
         and GROUP * width == LANES
         and taps == GROUP
         and blocks % GROUP == 0
-        and 2 * blocks <= LANES
+        and blocks <= LANES // 2
+        and width % 4 == 0
         and stations % 16 == 0
         and samples % 512 == 0
         and lax.axis_size("pol") == 2

time: 55.4 us -> 36.8 us (0.66)
  local copies, waits for them, and re-layouts: 17.3 us -> 3.29 us
  Pallas kernels: 37.7 us -> 33.2 us
    unnamed x8 -> x10, local copies, waits for them, and re-layouts: 17.3 us -> 3.29 us
    pallas_call x1, Pallas kernels: 7.73 us -> 4.07 us  [fast_body(): pl.pallas_call(functools.partial(correlate_kernel, blocks, capacity), out...]
    pallas_call x1, Pallas kernels: 30 us -> 29.1 us  [fast_body(): pl.pallas_call(functools.partial(channelize_kernel, sizes), out_shape=jax...]
where the time goes in v2:
time: 36.8 us; the launch traced here: 36.5 us
  Pallas kernels  33.2 us (90%)
  local copies, waits for them, and re-layouts  3.29 us (9%)
    pallas_call x1, Pallas kernels, fast_body(): pl.pallas_call(functools.partial(channelize_kernel, sizes), out_shape=jax...  29.1 us
    pallas_call x1, Pallas kernels, fast_body(): pl.pallas_call(functools.partial(correlate_kernel, blocks, capacity), out...  4.07 us
    unnamed x10, local copies, waits for them, and re-layouts  3.29 us

profile of v2, /device:TPU:0, one launch (start us, length us, event | category | flops | bytes accessed | tf_op | source)
XLA Modules:
  0.0 36.5 jit_solution(11151706192650678945)
XLA Ops:
  0.0 0.0 copy-start.1
  0.0 1.2 %copy-done.1 = bf16[4096,128]{1,0:T(8,128)(2,1)S(1)} copy-done((bf16[4096,128]{1,0:T(8,128)(2,1)S(1)}, bf16[4096,128]{1,0:T(8,128)(2,1)}, u32[]{:S(2)}) %copy-start.1) | copy-done | bytes 1048600
  1.2 0.0 copy-start.2
  1.2 0.8 %copy-done.2 = bf16[8,2048]{1,0:T(8,128)(2,1)S(1)} copy-done((bf16[8,2048]{1,0:T(8,128)(2,1)S(1)}, bf16[8,2048]{1,0:T(8,128)(2,1)}, u32[]{:S(2)}) %copy-start.2) | copy-done | bytes 32792
  2.0 0.0 copy-start.3
  2.0 0.7 %copy-done.3 = s32[32,1]{0,1:T(1,128)S(1)} copy-done((s32[32,1]{0,1:T(1,128)S(1)}, s32[32,1]{0,1:T(1,128)}, u32[]{:S(2)}) %copy-start.3) | copy-done | bytes 152
  2.6 0.0 copy-start.4
  2.6 0.7 %copy-done.4 = s32[32]{0:T(128)S(1)} copy-done((s32[32]{0:T(128)S(1)}, s32[32]{0:T(128)}, u32[]{:S(2)}) %copy-start.4) | copy-done | bytes 152
  3.3 0.0 copy-start
  3.3 29.1 %channelize.1.x_ref = bf16[2,256,768]{2,1,0:T(8,128)(2,1)S(1)} custom-call(bf16[55,32,4096]{2,1,0:T(8,128)(2,1)} %bitcast.7, bf16[8,2048]{1,0:T(8,128)(2,1)S(1)} %copy-done.2, bf16[4096,128]{1,0:T(8,128)(2,1)S(1)} %copy-done.1, s32[1,32]{1,0:T(1,128)S(1)} %bitcast.5, s32[1,32]{1,0:T(1,128)S(1)} %bitcast.6), custom_call_target="tpu_custom_call" | custom-call | tf_op jit(solution)/shard_map/channelize/pallas_call | solution.py:338
  32.4 0.0 copy-done
  32.4 4.1 %correlate.1 = bf16[1,8,2,256,512]{4,3,2,1,0:T(8,128)(2,1)} custom-call(bf16[2,256,768]{2,1,0:T(8,128)(2,1)S(1)} %channelize.1.x_ref, bf16[768,1024]{1,0:T(8,128)(2,1)S(1)} %copy-done), custom_call_target="tpu_custom_call" | custom-call | tf_op jit(solution)/shard_map/correlate/pallas_call | solution.py:365
Async XLA Ops:
  0.0 1.2 %copy-start.1 = (bf16[4096,128]{1,0:T(8,128)(2,1)S(1)}, bf16[4096,128]{1,0:T(8,128)(2,1)}, u32[]{:S(2)}) copy-start(bf16[4096,128]{1,0:T(8,128)(2,1)} %constant.4.clone.table_ref) | copy-start | bytes 3145732
  1.2 0.8 %copy-start.2 = (bf16[8,2048]{1,0:T(8,128)(2,1)S(1)}, bf16[8,2048]{1,0:T(8,128)(2,1)}, u32[]{:S(2)}) copy-start(bf16[8,2048]{1,0:T(8,128)(2,1)} %taps_ref.1) | copy-start | bytes 98308
  2.0 0.7 %copy-start.3 = (s32[32,1]{0,1:T(1,128)S(1)}, s32[32,1]{0,1:T(1,128)}, u32[]{:S(2)}) copy-start(s32[32,1]{0,1:T(1,128)} %param.8) | copy-start | bytes 388
  2.6 0.7 %copy-start.4 = (s32[32]{0:T(128)S(1)}, s32[32]{0:T(128)}, u32[]{:S(2)}) copy-start(s32[32]{0:T(128)} %param.9) | copy-start | bytes 388
  3.3 29.1 %copy-start = (bf16[768,1024]{1,0:T(8,128)(2,1)S(1)}, bf16[768,1024]{1,0:T(8,128)(2,1)}, u32[]{:S(2)}) copy-start(bf16[768,1024]{1,0:T(8,128)(2,1)} %constant.5.clone.place_ref) | copy-start | bytes 4718596

commit v3 on v2

--- a/solution.py
+++ b/solution.py
@@ -152,8 +152,8 @@
 
 
 def channelize_kernel(
-    sizes, v_ref, taps_ref, table_ref, owner_ref, marks_ref, x_ref,
-    vbuf, wbuf, zbuf, sendbuf, in_sem, send_sem, recv_sem, own_sem, pass_send, pass_recv,
+    sizes, v_ref, taps_hbm, table_hbm, owner_hbm, marks_hbm, x_ref,
+    taps_ref, table_ref, owner_ref, marks_ref, small_sem, vbuf, wbuf, zbuf, sendbuf, in_sem, send_sem, recv_sem, own_sem, pass_send, pass_recv,
 ):
     stations, span, samples, taps, blocks, channels, owners, capacity, tm_count = sizes
     cuts = row_cuts(blocks // GROUP)
@@ -163,6 +163,15 @@
     me = lax.axis_index("stn") * tm_count + lax.axis_index("tm")
     ends = [0] + [cut * GROUP + taps - 1 for cut in cuts[1:]]
 
+    small = [
+        pltpu.make_async_copy(source, target, small_sem.at[i])
+        for i, (source, target) in enumerate((
+            (taps_hbm, taps_ref), (table_hbm, table_ref), (owner_hbm, owner_ref),
+            (marks_hbm, marks_ref),
+        ))
+    ]
+    for load in small:
+        load.start()
     loads = []
     for c in range(steps):
         rows = pl.ds(ends[c], ends[c + 1] - ends[c])
@@ -181,6 +190,8 @@
         barrier, inc=1, device_id={"pol": 1 - pol}, device_id_type=pl.DeviceIdType.MESH
     )
 
+    for load in small:
+        load.wait()
     columns = taps * 2 * channels
     expand = jnp.where(
         iota((taps, columns), 0) == iota((taps, columns), 1) // (2 * channels), 1.0, 0.0
@@ -217,8 +228,7 @@
     sends, passes = [], []
 
     def send_groups(c, first, last):
-        lanes = pl.ds(first * LANES, (last - first) * LANES)
-        rows = pl.ds(me * stations, stations)
+        batch_groups = pl.ds(first, last - first)
         for g in range(first, last):
             summed = [shifted(g * GROUP + i) for i in range(GROUP + 1)]
             spectra = [
@@ -230,13 +240,13 @@
             )
             parts = [placed[i * stations : (i + 1) * stations] for i in range(GROUP)]
             for o, part in enumerate(block_transpose(parts, width)):
-                sendbuf[o, :, g * LANES : (g + 1) * LANES] = part.astype(jnp.bfloat16)
+                sendbuf[o, g] = part.astype(jnp.bfloat16)
         batch = []
         for k in range(1, owners):
             peer = lax.rem(me + k, owners)
             copy = pltpu.make_async_remote_copy(
-                src_ref=sendbuf.at[peer, :, lanes],
-                dst_ref=x_ref.at[pol, rows, lanes],
+                src_ref=sendbuf.at[peer, batch_groups],
+                dst_ref=x_ref.at[pol, me, batch_groups],
                 send_sem=send_sem.at[c, k],
                 recv_sem=recv_sem.at[c, k],
                 device_id={"stn": peer // tm_count, "tm": lax.rem(peer, tm_count)},
@@ -245,19 +255,19 @@
             copy.start()
             batch.append(copy)
         own = pltpu.make_async_copy(
-            sendbuf.at[me, :, lanes], x_ref.at[pol, rows, lanes], own_sem.at[c]
+            sendbuf.at[me, batch_groups], x_ref.at[pol, me, batch_groups], own_sem.at[c]
         )
         own.start()
-        sends.append((batch, own, lanes))
+        sends.append((batch, own, batch_groups))
 
     def pass_on(c):
-        batch, own, lanes = sends[c]
+        batch, own, batch_groups = sends[c]
         own.wait()
         for k in range(1, owners):
             source = lax.rem(me + owners - k, owners)
-            here = x_ref.at[pol, pl.ds(source * stations, stations), lanes]
+            here = x_ref.at[pol, source, batch_groups]
             pltpu.make_async_copy(here, here, recv_sem.at[c, k]).wait()
-        mine = x_ref.at[pol, :, lanes]
+        mine = x_ref.at[pol, :, batch_groups]
         copy = pltpu.make_async_remote_copy(
             src_ref=mine, dst_ref=mine, send_sem=pass_send.at[c], recv_sem=pass_recv.at[c],
             device_id={"pol": 1 - pol}, device_id_type=pl.DeviceIdType.MESH,
@@ -272,11 +282,10 @@
             vbuf[first:last].reshape((last - first) * stations, samples), wbuf[...],
             preferred_element_type=jnp.float32,
         )
-        if c >= 1:
-            pass_on(c - 1)
         send_groups(c, cuts[c], cuts[c + 1])
-    pass_on(steps - 1)
-    for batch, own, lanes in sends:
+    for c in range(steps):
+        pass_on(c)
+    for batch, own, batch_groups in sends:
         for copy in batch:
             copy.wait_send()
     for copy in passes:
@@ -293,8 +302,11 @@
 
 def correlate_kernel(blocks, capacity, x_ref, place_ref, out_ref, held, result, out_sem):
     pol = lax.axis_index("pol")
-    rows, depth = x_ref.shape[1], x_ref.shape[2]
-    signal = x_ref[...].reshape(2 * rows, depth)
+    _, owners, groups, stations, _ = x_ref.shape
+    rows = owners * stations
+    signal = jnp.concatenate(
+        [x_ref[:, :, g].reshape(2 * rows, LANES) for g in range(groups)], axis=1
+    )
     sign = jnp.where(iota((1, LANES), 1) < LANES // 2, 1.0, -1.0)
     copies = []
     for pair in range(capacity // 2):
@@ -329,22 +341,27 @@
     tm_count = lax.axis_size("tm")
     owners = lax.axis_size("stn") * tm_count
     capacity = 2 * channels // owners
-    steps = len(row_cuts(blocks // GROUP)) - 1
-    lanes = blocks * 2 * capacity
+    groups = blocks // GROUP
+    steps = len(row_cuts(groups)) - 1
     columns = taps * 2 * channels
     sizes = (stations, span, samples, taps, blocks, channels, owners, capacity, tm_count)
     vmem = pl.BlockSpec(memory_space=pltpu.VMEM)
     dma = pltpu.SemaphoreType.DMA
     x = pl.pallas_call(
         functools.partial(channelize_kernel, sizes),
-        out_shape=jax.ShapeDtypeStruct((2, owners * stations, lanes), jnp.bfloat16),
-        in_specs=[pl.BlockSpec(memory_space=pl.ANY), vmem, vmem, vmem, vmem],
+        out_shape=jax.ShapeDtypeStruct((2, owners, groups, stations, LANES), jnp.bfloat16),
+        in_specs=[pl.BlockSpec(memory_space=pltpu.HBM)] * 5,
         out_specs=vmem,
         scratch_shapes=[
+            pltpu.VMEM(fir_taps.shape, jnp.bfloat16),
+            pltpu.VMEM((samples, LANES), jnp.bfloat16),
+            pltpu.VMEM((1, channels), jnp.int32),
+            pltpu.VMEM((1, stations), jnp.int32),
+            dma((4,)),
             pltpu.VMEM((span, stations, samples), jnp.bfloat16),
             pltpu.VMEM((samples, columns), jnp.bfloat16),
             pltpu.VMEM((span * stations, columns), jnp.float32),
-            pltpu.VMEM((owners, stations, lanes), jnp.bfloat16),
+            pltpu.VMEM((owners, groups, stations, LANES), jnp.bfloat16),
             dma((steps,)),
             dma((steps, owners)),
             dma((steps, owners)),
@@ -353,7 +370,7 @@
             dma((steps,)),
         ],
         compiler_params=pltpu.CompilerParams(
-            collective_id=0, has_side_effects=True, vmem_limit_bytes=52 * 1024 * 1024
+            collective_id=0, has_side_effects=True, vmem_limit_bytes=48 * 1024 * 1024
         ),
         name="channelize",
     )(

time: 36.8 us -> 29.5 us (0.80)
  Pallas kernels: 33.2 us -> 26 us
    pallas_call x1, Pallas kernels: 29.1 us -> 21.9 us  [fast_body(): pl.pallas_call(functools.partial(channelize_kernel, sizes), out_shape=jax...]
where the time goes in v3:
time: 29.5 us; the launch traced here: 29.3 us
  Pallas kernels  26 us (88%)
  local copies, waits for them, and re-layouts  3.29 us (11%)
    pallas_call x1, Pallas kernels, fast_body(): pl.pallas_call(functools.partial(channelize_kernel, sizes), out_shape=jax...  21.9 us
    pallas_call x1, Pallas kernels, fast_body(): pl.pallas_call(functools.partial(correlate_kernel, blocks, capacity), out...  4.07 us
    unnamed x10, local copies, waits for them, and re-layouts  3.29 us

profile of v3, /device:TPU:0, one launch (start us, length us, event | category | flops | bytes accessed | tf_op | source)
XLA Modules:
  0.0 29.3 jit_solution(2897520576127510817)
XLA Ops:
  0.0 0.0 copy-start.1
  0.0 1.2 %copy-done.1 = bf16[4096,128]{1,0:T(8,128)(2,1)S(1)} copy-done((bf16[4096,128]{1,0:T(8,128)(2,1)S(1)}, bf16[4096,128]{1,0:T(8,128)(2,1)}, u32[]{:S(2)}) %copy-start.1) | copy-done | bytes 1048600
  1.2 0.0 copy-start.2
  1.2 0.8 %copy-done.2 = bf16[8,2048]{1,0:T(8,128)(2,1)S(1)} copy-done((bf16[8,2048]{1,0:T(8,128)(2,1)S(1)}, bf16[8,2048]{1,0:T(8,128)(2,1)}, u32[]{:S(2)}) %copy-start.2) | copy-done | bytes 32792
  2.0 0.0 copy-start.3
  2.0 0.7 %copy-done.3 = s32[32,1]{0,1:T(1,128)S(1)} copy-done((s32[32,1]{0,1:T(1,128)S(1)}, s32[32,1]{0,1:T(1,128)}, u32[]{:S(2)}) %copy-start.3) | copy-done | bytes 152
  2.6 0.0 copy-start.4
  2.6 0.7 %copy-done.4 = s32[32]{0:T(128)S(1)} copy-done((s32[32]{0:T(128)S(1)}, s32[32]{0:T(128)}, u32[]{:S(2)}) %copy-start.4) | copy-done | bytes 152
  3.3 0.0 copy-start
  3.3 21.9 %channelize.1.x_ref = bf16[2,8,6,32,128]{4,3,2,1,0:T(8,128)(2,1)S(1)} custom-call(bf16[55,32,4096]{2,1,0:T(8,128)(2,1)} %bitcast.7, bf16[8,2048]{1,0:T(8,128)(2,1)S(1)} %copy-done.2, bf16[4096,128]{1,0:T(8,128)(2,1)S(1)} %copy-done.1, s32[1,32]{1,0:T(1,128)S(1)} %bitcast.5, s32[1,32]{1,0:T(1,128)S(1)} %bitcast.6), custom_call_target="tpu_custom_call" | custom-call | tf_op jit(solution)/shard_map/channelize/pallas_call | solution.py:350
  25.2 0.0 copy-done
  25.2 4.1 %correlate.1 = bf16[1,8,2,256,512]{4,3,2,1,0:T(8,128)(2,1)} custom-call(bf16[2,8,6,32,128]{4,3,2,1,0:T(8,128)(2,1)S(1)} %channelize.1.x_ref, bf16[768,1024]{1,0:T(8,128)(2,1)S(1)} %copy-done), custom_call_target="tpu_custom_call" | custom-call | tf_op jit(solution)/shard_map/correlate/pallas_call | solution.py:382
Async XLA Ops:
  0.0 1.2 %copy-start.1 = (bf16[4096,128]{1,0:T(8,128)(2,1)S(1)}, bf16[4096,128]{1,0:T(8,128)(2,1)}, u32[]{:S(2)}) copy-start(bf16[4096,128]{1,0:T(8,128)(2,1)} %constant.4.clone.table_hbm) | copy-start | bytes 3145732
  1.2 0.8 %copy-start.2 = (bf16[8,2048]{1,0:T(8,128)(2,1)S(1)}, bf16[8,2048]{1,0:T(8,128)(2,1)}, u32[]{:S(2)}) copy-start(bf16[8,2048]{1,0:T(8,128)(2,1)} %taps_hbm.1) | copy-start | bytes 98308
  2.0 0.7 %copy-start.3 = (s32[32,1]{0,1:T(1,128)S(1)}, s32[32,1]{0,1:T(1,128)}, u32[]{:S(2)}) copy-start(s32[32,1]{0,1:T(1,128)} %param.8) | copy-start | bytes 388
  2.6 0.7 %copy-start.4 = (s32[32]{0:T(128)S(1)}, s32[32]{0:T(128)}, u32[]{:S(2)}) copy-start(s32[32]{0:T(128)} %param.9) | copy-start | bytes 388
  3.3 21.9 %copy-start = (bf16[768,1024]{1,0:T(8,128)(2,1)S(1)}, bf16[768,1024]{1,0:T(8,128)(2,1)}, u32[]{:S(2)}) copy-start(bf16[768,1024]{1,0:T(8,128)(2,1)} %constant.5.clone.place_ref) | copy-start | bytes 4718596

commit v4 on v3

--- a/solution.py
+++ b/solution.py
@@ -176,8 +176,8 @@
     for c in range(steps):
         rows = pl.ds(ends[c], ends[c + 1] - ends[c])
         load = pltpu.make_async_copy(v_ref.at[rows], vbuf.at[rows], in_sem.at[c])
-        load.start()
         loads.append(load)
+    loads[0].start()
 
     barrier = pltpu.get_barrier_semaphore()
     for k in range(1, owners):
@@ -192,6 +192,7 @@
 
     for load in small:
         load.wait()
+    loads[1].start()
     columns = taps * 2 * channels
     expand = jnp.where(
         iota((taps, columns), 0) == iota((taps, columns), 1) // (2 * channels), 1.0, 0.0
@@ -210,6 +211,8 @@
                 lanes = slice(j * LANES, (j + 1) * LANES)
                 wbuf[at, lanes] = (tap_rows[:, lanes] * entry).astype(jnp.bfloat16)
 
+    for load in loads[2:]:
+        load.start()
     pick = slot_columns(owner_ref, channels, capacity)
     diagonal = iota((stations, stations), 0) == iota((stations, stations), 1)
     keep = 1.0 - jnp.sum(
@@ -292,43 +295,33 @@
         copy.wait()
 
 
-def lane_places(blocks, capacity):
-    table = np.zeros((blocks, capacity, 2, capacity, 2, LANES // 2), np.float32)
-    for k in range(capacity):
-        for q in range(2):
-            table[np.arange(blocks), k, q, k, q, np.arange(blocks)] = 1.0
-    return table.reshape(blocks * capacity * 2, capacity * LANES).astype(jnp.bfloat16)
-
-
-def correlate_kernel(blocks, capacity, x_ref, place_ref, out_ref, held, result, out_sem):
+def correlate_kernel(blocks, capacity, x_ref, out_ref, held, result, out_sem):
     pol = lax.axis_index("pol")
     _, owners, groups, stations, _ = x_ref.shape
     rows = owners * stations
-    signal = jnp.concatenate(
-        [x_ref[:, :, g].reshape(2 * rows, LANES) for g in range(groups)], axis=1
-    )
-    sign = jnp.where(iota((1, LANES), 1) < LANES // 2, 1.0, -1.0)
+    lane = iota((1, LANES), 1)
+    straight, turned = [], []
+    for g in range(groups):
+        every = x_ref[:, :, g].reshape(2 * rows, LANES).astype(jnp.float32)
+        held[g * LANES : (g + 1) * LANES, :] = every.T.astype(jnp.bfloat16)
+        left = x_ref[pol, :, g].reshape(rows, LANES)
+        wide = left.astype(jnp.float32)
+        swapped = jnp.where(
+            lane % 2 == 0, pltpu.roll(wide, LANES - 1, 1), -pltpu.roll(wide, 1, 1)
+        )
+        straight.append(left)
+        turned.append(swapped.astype(jnp.bfloat16))
+    operands = [jnp.concatenate(tiles, axis=1) for tiles in (straight, turned)]
+    lane = iota((1, groups * LANES), 1)
     copies = []
-    for pair in range(capacity // 2):
-        lanes = slice(pair * 2 * LANES, (pair + 1) * 2 * LANES)
-        held[:, :, lanes] = (
-            jnp.dot(signal, place_ref[:, lanes], preferred_element_type=jnp.float32)
-            .astype(jnp.bfloat16)
-            .reshape(2, rows, 2 * LANES)
-        )
-        for k in (2 * pair, 2 * pair + 1):
-            lanes = slice(k * LANES, (k + 1) * LANES)
-            right = held[:, :, lanes].reshape(2 * rows, LANES)
-            left = held[pol, :, lanes]
-            turned = pltpu.roll(left.astype(jnp.float32), LANES // 2, 1) * sign
-            for q, operand in enumerate((left, turned.astype(jnp.bfloat16))):
-                product = lax.dot_general(
-                    operand, right, (((1,), (1,)), ((), ())), preferred_element_type=jnp.float32
-                )
-                result[k, q] = (product * (1.0 / blocks)).astype(jnp.bfloat16)
-            copy = pltpu.make_async_copy(result.at[k], out_ref.at[0, k], out_sem.at[k])
-            copy.start()
-            copies.append(copy)
+    for k in range(capacity):
+        mask = jnp.where(lane % (2 * capacity) // 2 == k, 1.0, 0.0).astype(jnp.bfloat16)
+        for q, operand in enumerate(operands):
+            product = jnp.dot(operand * mask, held[...], preferred_element_type=jnp.float32)
+            result[k, q] = (product * (1.0 / blocks)).astype(jnp.bfloat16)
+        copy = pltpu.make_async_copy(result.at[k], out_ref.at[0, k], out_sem.at[k])
+        copy.start()
+        copies.append(copy)
     for copy in copies:
         copy.wait()
 
@@ -370,7 +363,7 @@
             dma((steps,)),
         ],
         compiler_params=pltpu.CompilerParams(
-            collective_id=0, has_side_effects=True, vmem_limit_bytes=48 * 1024 * 1024
+            collective_id=0, has_side_effects=True, vmem_limit_bytes=60 * 1024 * 1024
         ),
         name="channelize",
     )(
@@ -382,16 +375,16 @@
     return pl.pallas_call(
         functools.partial(correlate_kernel, blocks, capacity),
         out_shape=jax.ShapeDtypeStruct((1, capacity, 2, rows, 2 * rows), jnp.bfloat16),
-        in_specs=[vmem, vmem],
+        in_specs=[vmem],
         out_specs=pl.BlockSpec(memory_space=pl.ANY),
         scratch_shapes=[
-            pltpu.VMEM((2, rows, capacity * LANES), jnp.bfloat16),
+            pltpu.VMEM((groups * LANES, 2 * rows), jnp.bfloat16),
             pltpu.VMEM((capacity, 2, rows, 2 * rows), jnp.bfloat16),
             dma((capacity,)),
         ],
         compiler_params=pltpu.CompilerParams(vmem_limit_bytes=24 * 1024 * 1024),
         name="correlate",
-    )(x, jnp.asarray(lane_places(blocks, capacity)))
+    )(x)
 
 
 def body(voltages, fir_taps, owner_map, station_flag_marks):
@@ -409,6 +402,7 @@
         and blocks % GROUP == 0
         and blocks <= LANES // 2
         and width % 4 == 0
+        and blocks >= 2 * GROUP
         and stations % 16 == 0
         and samples % 512 == 0
         and lax.axis_size("pol") == 2

time: 29.5 us -> 28.7 us (0.973)
  local copies, waits for them, and re-layouts: 3.29 us -> 1.13 us
  Pallas kernels: 26 us -> 27.4 us
    unnamed x10 -> x2, local copies, waits for them, and re-layouts: 3.29 us -> 1.13 us
    pallas_call x1, Pallas kernels: 21.9 us -> 23 us  [fast_body(): pl.pallas_call(functools.partial(channelize_kernel, sizes), out_shape=jax...]
    pallas_call x1, Pallas kernels: 4.07 us -> 4.4 us  [fast_body(): pl.pallas_call(functools.partial(correlate_kernel, blocks, capacity), out...]
where the time goes in v4:
time: 28.7 us; the launch traced here: 28.5 us
  Pallas kernels  27.4 us (95%)
  local copies, waits for them, and re-layouts  1.13 us (4%)
    pallas_call x1, Pallas kernels, fast_body(): pl.pallas_call(functools.partial(channelize_kernel, sizes), out_shape=jax...  23 us
    pallas_call x1, Pallas kernels, fast_body(): pl.pallas_call(functools.partial(correlate_kernel, blocks, capacity), out...  4.4 us
    unnamed x2, local copies, waits for them, and re-layouts  1.13 us

profile of v4, /device:TPU:0, one launch (start us, length us, event | category | flops | bytes accessed | tf_op | source)
XLA Modules:
  0.0 28.5 jit_solution(11617163683541096017)
XLA Ops:
  0.0 23.0 %channelize.1.x_ref = bf16[2,8,6,32,128]{4,3,2,1,0:T(8,128)(2,1)} custom-call(bf16[55,32,4096]{2,1,0:T(8,128)(2,1)} %bitcast.5, bf16[8,2048]{1,0:T(8,128)(2,1)} %taps_hbm.1, bf16[4096,128]{1,0:T(8,128)(2,1)} %constant.2.clone.table_hbm, s32[1,32]{1,0:T(1,128)} %bitcast.6, s32[1,32]{1,0:T(1,128)} %bitcast.7), custom_call_target="tpu_custom_call" | custom-call | tf_op jit(solution)/shard_map/channelize/pallas_call | solution.py:343
  23.0 0.0 copy-start
  23.0 1.1 %copy-done = bf16[2,8,6,32,128]{4,3,2,1,0:T(8,128)(2,1)S(1)} copy-done((bf16[2,8,6,32,128]{4,3,2,1,0:T(8,128)(2,1)S(1)}, bf16[2,8,6,32,128]{4,3,2,1,0:T(8,128)(2,1)}, u32[]{:S(2)}) %copy-start) | copy-done | bytes 786456
  24.1 4.4 %correlate.1 = bf16[1,8,2,256,512]{4,3,2,1,0:T(8,128)(2,1)} custom-call(bf16[2,8,6,32,128]{4,3,2,1,0:T(8,128)(2,1)S(1)} %copy-done), custom_call_target="tpu_custom_call" | custom-call | tf_op jit(solution)/shard_map/correlate/pallas_call | solution.py:375
Async XLA Ops:
  23.0 1.1 %copy-start = (bf16[2,8,6,32,128]{4,3,2,1,0:T(8,128)(2,1)S(1)}, bf16[2,8,6,32,128]{4,3,2,1,0:T(8,128)(2,1)}, u32[]{:S(2)}) copy-start(bf16[2,8,6,32,128]{4,3,2,1,0:T(8,128)(2,1)} %channelize.1.x_ref) | copy-start | bytes 2359300

commit v5 on v4

--- a/solution.py
+++ b/solution.py
@@ -286,7 +286,9 @@
             preferred_element_type=jnp.float32,
         )
         send_groups(c, cuts[c], cuts[c + 1])
-    for c in range(steps):
+        if c >= 2:
+            pass_on(c - 2)
+    for c in range(max(steps - 2, 0), steps):
         pass_on(c)
     for batch, own, batch_groups in sends:
         for copy in batch:

time: 28.7 us -> 28.7 us (level)
  no operation moved by 1% of the time
where the time goes in v5:
time: 28.7 us; the launch traced here: 28.5 us
  Pallas kernels  27.4 us (95%)
  local copies, waits for them, and re-layouts  1.13 us (4%)
    pallas_call x1, Pallas kernels, fast_body(): pl.pallas_call(functools.partial(channelize_kernel, sizes), out_shape=jax...  23 us
    pallas_call x1, Pallas kernels, fast_body(): pl.pallas_call(functools.partial(correlate_kernel, blocks, capacity), out...  4.4 us
    unnamed x2, local copies, waits for them, and re-layouts  1.13 us

profile of v5, /device:TPU:0, one launch (start us, length us, event | category | flops | bytes accessed | tf_op | source)
XLA Modules:
  0.0 28.5 jit_solution(11777673455187081514)
XLA Ops:
  0.0 23.0 %channelize.1.x_ref = bf16[2,8,6,32,128]{4,3,2,1,0:T(8,128)(2,1)} custom-call(bf16[55,32,4096]{2,1,0:T(8,128)(2,1)} %bitcast.5, bf16[8,2048]{1,0:T(8,128)(2,1)} %taps_hbm.1, bf16[4096,128]{1,0:T(8,128)(2,1)} %constant.2.clone.table_hbm, s32[1,32]{1,0:T(1,128)} %bitcast.6, s32[1,32]{1,0:T(1,128)} %bitcast.7), custom_call_target="tpu_custom_call" | custom-call | tf_op jit(solution)/shard_map/channelize/pallas_call | solution.py:345
  23.0 0.0 copy-start
  23.0 1.1 %copy-done = bf16[2,8,6,32,128]{4,3,2,1,0:T(8,128)(2,1)S(1)} copy-done((bf16[2,8,6,32,128]{4,3,2,1,0:T(8,128)(2,1)S(1)}, bf16[2,8,6,32,128]{4,3,2,1,0:T(8,128)(2,1)}, u32[]{:S(2)}) %copy-start) | copy-done | bytes 786456
  24.1 4.4 %correlate.1 = bf16[1,8,2,256,512]{4,3,2,1,0:T(8,128)(2,1)} custom-call(bf16[2,8,6,32,128]{4,3,2,1,0:T(8,128)(2,1)S(1)} %copy-done), custom_call_target="tpu_custom_call" | custom-call | tf_op jit(solution)/shard_map/correlate/pallas_call | solution.py:377
Async XLA Ops:
  23.0 1.1 %copy-start = (bf16[2,8,6,32,128]{4,3,2,1,0:T(8,128)(2,1)S(1)}, bf16[2,8,6,32,128]{4,3,2,1,0:T(8,128)(2,1)}, u32[]{:S(2)}) copy-start(bf16[2,8,6,32,128]{4,3,2,1,0:T(8,128)(2,1)} %channelize.1.x_ref) | copy-start | bytes 2359300
